TPU v7x, 32 devices: a whole 2x2x4 slice. The times are simulated.
32 devices in a mesh: blk: 8 (over y, x, core), col: 4 (over z).
Axes of the slice: x: 2, y: 2, z: 4, core: 2. Of those that a mesh axis runs over, the one named last changes fastest.
Arguments:
- src_feat: bfloat16 [16, 1024, 256], P('blk', 'col'), may hold values from -40 to 40
- tgt_feat: bfloat16 [16, 1024, 256], P('blk', 'col'), may hold values from -40 to 40
- src_mass: bfloat16 [16, 1024], P('blk', 'col'), may hold values from 0.5 to 2
- tgt_mass: bfloat16 [16, 1024], P('blk', 'col'), may hold values from 0.5 to 2
- candidates: int32 [16, 8], P('blk'), may hold values from 0 to 15, as said below
- counts: int32 [16], P('blk'), may hold values from 1 to 8, as said below
- tgt_home: int32 [16], replicated, may hold values from 0 to 15, each once
Outputs:
- src_aligned: bfloat16 [16, 1024, 256], P('blk', 'col')
- tgt_aligned: bfloat16 [16, 1024, 256], P('blk', 'col')
Inputs may be any that keep to these rules, and one draw needn't show every extreme that they name: `candidates`: each row's 8 entries are distinct; the first counts[i] of row i are live, the others are not used; every target block number is among the live entries of some row. `counts`: the 2 blocks of one index of blk hold at most 12 live slots together, and the blocks of some index hold exactly 12. A permutation: target block number j is stored as block tgt_home[j] of tgt_feat and tgt_mass.
All inputs are finite; a program needn't handle non-finite values.
Results may differ from a plain program's by a relative error of at most 0.017.
Values may be sent and summed in bfloat16 or wider, within the bound.
A program may use at most 64 MiB of HBM per device.

v0:
```python
import functools
import math

import jax
import jax.numpy as jnp
from jax import lax
from jax.experimental import pallas as pl
from jax.experimental.pallas import tpu as pltpu
from jax.sharding import PartitionSpec as P

ITERS = 2
PAIRS = 12
MESH = pl.DeviceIdType.MESH
F32, BF16 = jnp.float32, jnp.bfloat16
LOG2E = math.log2(math.e)
SCALE = LOG2E / 0.02
SHIFT = -0.3 * LOG2E / 0.02
DEAD = -1e30
NT = (((1,), (1,)), ((), ()))


def unit_rows(values):
    inverse = lax.rsqrt(jnp.mean(values * values, axis=-1, keepdims=True) + 1e-6)
    return (values * inverse).astype(BF16)


def split_rows(row):
    wide = jnp.broadcast_to(row, (16, row.shape[1]))
    high = wide.astype(BF16).astype(F32)
    first = lax.broadcasted_iota(jnp.int32, wide.shape, 0) < 8
    return jnp.where(first, high, wide - high).astype(BF16)


def column_of(row, width):
    turned = jnp.transpose(jnp.broadcast_to(row, (128, row.shape[1])))
    return jnp.concatenate([turned] * (width // 128), axis=1)


def kernel(nb_dev, nc, src_ref, tgt_ref, smass_ref, tmass_ref, cand_ref, count_ref, home_ref,
           src_out, tgt_out, src_all, src_unit, src_turned, tgt_all, kmat, smass_all, tmass_all,
           u_rep, v_rep, row_parts, col_parts, row_tot, col_tot, back, acc, src_send, src_recv,
           tgt_send, tgt_recv, slot_src, slot_tgt, slot_bias, pair_slot,
           col_ss, col_rs, blk_ss, blk_rs):
    b, c = lax.axis_index("blk"), lax.axis_index("col")
    local_blocks, sub, width = src_ref.shape
    slot_max = cand_ref.shape[1]
    blocks = tgt_all.shape[0]
    full = src_all.shape[1]

    barrier = pltpu.get_barrier_semaphore()
    for d in range(1, nc):
        pl.semaphore_signal(barrier, inc=1, device_id={"col": lax.rem(c + d, nc)}, device_id_type=MESH)
    for d in range(1, nb_dev):
        pl.semaphore_signal(barrier, inc=1, device_id={"blk": lax.rem(b + d, nb_dev)}, device_id_type=MESH)
    pl.semaphore_wait(barrier, nc + nb_dev - 2)

    def to_col(kind, source, target):
        out = []
        for d in range(1, nc):
            peer = lax.rem(c + d, nc)
            copy = pltpu.make_async_remote_copy(
                src_ref=source(peer), dst_ref=target, send_sem=col_ss.at[kind, d],
                recv_sem=col_rs.at[kind, d], device_id={"col": peer}, device_id_type=MESH)
            copy.start()
            out.append(copy)
        return out

    def to_blk(kind, source, target):
        out = []
        for d in range(1, nb_dev):
            peer = lax.rem(b + d, nb_dev)
            copy = pltpu.make_async_remote_copy(
                src_ref=source(peer), dst_ref=target, send_sem=blk_ss.at[kind, d],
                recv_sem=blk_rs.at[kind, d], device_id={"blk": peer}, device_id_type=MESH)
            copy.start()
            out.append(copy)
        return out

    def finish(copies):
        for copy in copies:
            copy.wait()

    my_rows = pl.ds(pl.multiple_of(c * sub, sub), sub)
    my_blocks = pl.ds(b * local_blocks, local_blocks)
    src_copies = to_col(0, lambda peer: src_ref, src_all.at[:, my_rows, :])
    tgt_copies = to_blk(0, lambda peer: tgt_ref, tgt_all.at[my_blocks])
    mass_copies = to_col(1, lambda peer: smass_ref, smass_all.at[c])
    mass_copies += to_blk(1, lambda peer: tmass_ref, tmass_all.at[my_blocks])
    src_all[:, my_rows, :] = src_ref[...]
    tgt_all[my_blocks] = tgt_ref[...]
    smass_all[c] = smass_ref[...]
    tmass_all[my_blocks] = tmass_ref[...]

    total = count_ref[0]
    for p in range(1, local_blocks):
        total = total + count_ref[p]
    for s in range(PAIRS):
        owner, start, end = 0, 0, count_ref[0]
        for p in range(1, local_blocks):
            owner = jnp.where(s >= end, p, owner)
            start = jnp.where(s >= end, end, start)
            end = end + count_ref[p]
        within = jnp.minimum(s - start, slot_max - 1)
        alive = s < total
        slot_src[s] = jnp.int32(owner)
        slot_tgt[s] = jnp.where(alive, home_ref[cand_ref[owner, within]], blocks)
        slot_bias[s] = jnp.where(alive, F32(SHIFT), F32(DEAD))

    @pl.loop(0, blocks)
    def _(n):
        for p in range(local_blocks):
            found = jnp.int32(PAIRS)
            for s in range(PAIRS):
                hit = jnp.logical_and(slot_src[s] == p, slot_tgt[s] == n)
                found = jnp.where(hit, s, found)
            pair_slot[n, p] = found

    back[PAIRS] = jnp.zeros(back.shape[1:], F32)
    acc[...] = jnp.zeros(acc.shape, F32)
    finish(src_copies)

    @pl.loop(0, nc)
    def _(piece):
        rows = pl.ds(pl.multiple_of(piece * sub, sub), sub)
        for p in range(local_blocks):
            values = src_all[p, rows, :].astype(F32)
            src_unit[p, rows, :] = unit_rows(values)
            src_turned[p, :, rows] = jnp.transpose(values).astype(BF16)

    finish(tgt_copies)

    row_ids = lax.broadcasted_iota(jnp.int32, (8, full), 0)
    block_ids = lax.broadcasted_iota(jnp.int32, (blocks, sub), 0)
    ones = jnp.where(lax.broadcasted_iota(jnp.int32, (16, sub), 0) < 8, F32(1), F32(0)).astype(BF16)

    def row_part(s, v_rows, running):
        found = lax.dot_general(v_rows, kmat[s], NT, preferred_element_type=F32)
        return running + jnp.where(row_ids == slot_src[s], found[:8] + found[8:], 0.0)

    def first_step(s, running):
        source, target = slot_src[s], jnp.minimum(slot_tgt[s], blocks - 1)
        bias = slot_bias[s]
        tile = unit_rows(tgt_all[target].astype(F32))
        chunk = 256
        for at in range(0, full, chunk):
            score = lax.dot_general(src_unit[source, at:at + chunk, :], tile, NT,
                                    preferred_element_type=F32)
            kmat[s, at:at + chunk, :] = jnp.exp2(score * F32(SCALE / width) + bias).astype(BF16)
        return row_part(s, ones, running)

    def later_step(s, running):
        return row_part(s, v_rep[jnp.minimum(slot_tgt[s], blocks - 1)], running)

    def col_step(s, running):
        found = jnp.dot(u_rep[slot_src[s]], kmat[s], preferred_element_type=F32)
        found = found[:8] + found[8:]
        return running + jnp.where(block_ids == slot_tgt[s], found[:1], 0.0)

    for step in range(ITERS):
        row_parts[step, c] = lax.fori_loop(
            0, PAIRS, first_step if step == 0 else later_step, jnp.zeros((8, full), F32))
        finish(to_col(2 + step, lambda peer: row_parts.at[step, c], row_parts.at[step, c]))
        rows = row_parts[step, 0]
        for at in range(1, nc):
            rows = rows + row_parts[step, at]
        rows = jnp.where(row_ids < local_blocks, rows, 1.0)
        row_tot[...] = rows
        if step == 0:
            finish(mass_copies)
        masses = jnp.concatenate([smass_all[at] for at in range(nc)], axis=1)
        scaling_u = masses / rows
        for p in range(local_blocks):
            u_rep[p] = split_rows(scaling_u[p:p + 1])
            if step == ITERS - 1:
                src_turned[p] = (src_turned[p].astype(F32) * scaling_u[p:p + 1]).astype(BF16)
        col_parts[step, b] = lax.fori_loop(0, PAIRS, col_step, jnp.zeros((blocks, sub), F32))
        col_copies = to_blk(2 + step, lambda peer: col_parts.at[step, b], col_parts.at[step, b])
        if step == ITERS - 1:
            @pl.loop(0, PAIRS)
            def _(s):
                back[s] = jnp.dot(src_turned[slot_src[s]], kmat[s], preferred_element_type=F32)

            @pl.loop(0, blocks)
            def _(n):
                piece = back[pair_slot[n, 0]]
                for p in range(1, local_blocks):
                    piece = piece + back[pair_slot[n, p]]
                tgt_send[n] = piece.astype(BF16)
        finish(col_copies)
        columns = col_parts[step, 0]
        for at in range(1, nb_dev):
            columns = columns + col_parts[step, at]
        col_tot[...] = columns
        if step == ITERS - 1:
            tgt_sums = to_blk(
                2 + ITERS, lambda peer: tgt_send.at[pl.ds(peer * local_blocks, local_blocks)],
                tgt_recv.at[b])

        @pl.loop(0, blocks)
        def _(n):
            row = tmass_all[n, :1, :] / col_tot[pl.ds(n, 1), :]
            if step < ITERS - 1:
                v_rep[n] = split_rows(row)
            else:
                tgt_all[n] = (tgt_all[n].astype(F32) * column_of(row, width)).astype(BF16)

    @pl.loop(0, PAIRS)
    def _(s):
        tile = tgt_all[jnp.minimum(slot_tgt[s], blocks - 1)]
        source = slot_src[s]
        chunk = 256
        for at in range(0, full, chunk):
            toward = jnp.dot(kmat[s, at:at + chunk, :], tile, preferred_element_type=F32)
            for p in range(local_blocks):
                hot = jnp.where(source == p, F32(1), F32(0))
                acc[p, at:at + chunk, :] += toward * hot

    for at in range(nc):
        src_send[at] = acc[:, at * sub:(at + 1) * sub, :].astype(BF16)
    src_sums = to_col(2 + ITERS, lambda peer: src_send.at[peer], src_recv.at[c])
    src_recv[c] = src_send[c]
    tgt_recv[b] = tgt_send[my_blocks]
    finish(src_sums)
    for p in range(local_blocks):
        whole = src_recv[0, p].astype(F32)
        for at in range(1, nc):
            whole = whole + src_recv[at, p].astype(F32)
        src_out[p] = (whole / column_of(row_tot[p:p + 1, my_rows], width)).astype(BF16)
    finish(tgt_sums)
    for q in range(local_blocks):
        whole = tgt_recv[0, q].astype(F32)
        for at in range(1, nb_dev):
            whole = whole + tgt_recv[at, q].astype(F32)
        whole = whole / col_tot[pl.ds(b * local_blocks + q, 1), :]
        tgt_out[q] = jnp.transpose(whole).astype(BF16)


def local(nb_dev, nc, src_feat, tgt_feat, src_mass, tgt_mass, candidates, counts, tgt_home):
    local_blocks, sub, width = src_feat.shape
    blocks = tgt_home.shape[0]
    full = sub * nc
    smass = jnp.pad(src_mass.astype(F32), ((0, 8 - local_blocks), (0, 0)))
    tmass = jnp.broadcast_to(tgt_mass.astype(F32)[:, None, :], (local_blocks, 8, sub))
    vmem = pl.BlockSpec(memory_space=pltpu.VMEM)
    smem = pl.BlockSpec(memory_space=pltpu.SMEM)
    kinds = 3 + ITERS
    shape = jax.ShapeDtypeStruct((local_blocks, sub, width), BF16)
    flops = 2 * PAIRS * full * sub * width * 3
    return pl.pallas_call(
        functools.partial(kernel, nb_dev, nc),
        out_shape=(shape, shape),
        in_specs=[vmem] * 4 + [smem] * 3,
        out_specs=(vmem, vmem),
        scratch_shapes=[
            pltpu.VMEM((local_blocks, full, width), BF16),
            pltpu.VMEM((local_blocks, full, width), BF16),
            pltpu.VMEM((local_blocks, width, full), BF16),
            pltpu.VMEM((blocks, sub, width), BF16),
            pltpu.VMEM((PAIRS, full, sub), BF16),
            pltpu.VMEM((nc, 8, sub), F32),
            pltpu.VMEM((blocks, 8, sub), F32),
            pltpu.VMEM((local_blocks, 16, full), BF16),
            pltpu.VMEM((blocks, 16, sub), BF16),
            pltpu.VMEM((ITERS, nc, 8, full), F32),
            pltpu.VMEM((ITERS, nb_dev, blocks, sub), F32),
            pltpu.VMEM((8, full), F32),
            pltpu.VMEM((blocks, sub), F32),
            pltpu.VMEM((PAIRS + 1, width, sub), F32),
            pltpu.VMEM((local_blocks, full, width), F32),
            pltpu.VMEM((nc, local_blocks, sub, width), BF16),
            pltpu.VMEM((nc, local_blocks, sub, width), BF16),
            pltpu.VMEM((blocks, width, sub), BF16),
            pltpu.VMEM((nb_dev, local_blocks, width, sub), BF16),
            pltpu.SMEM((PAIRS,), jnp.int32),
            pltpu.SMEM((PAIRS,), jnp.int32),
            pltpu.SMEM((PAIRS,), F32),
            pltpu.SMEM((blocks, local_blocks), jnp.int32),
            pltpu.SemaphoreType.DMA((kinds, nc)),
            pltpu.SemaphoreType.DMA((kinds, nc)),
            pltpu.SemaphoreType.DMA((kinds, nb_dev)),
            pltpu.SemaphoreType.DMA((kinds, nb_dev)),
        ],
        compiler_params=pltpu.CompilerParams(
            collective_id=0, has_side_effects=True, vmem_limit_bytes=56 * 1024 * 1024),
        cost_estimate=pl.CostEstimate(
            flops=flops, bytes_accessed=4 * local_blocks * sub * width * 2,
            transcendentals=PAIRS * full * sub),
    )(src_feat, tgt_feat, smass, tmass, candidates, counts, tgt_home)


def solution(mesh):
    in_specs = (
        P("blk", "col", None),
        P("blk", "col", None),
        P("blk", "col"),
        P("blk", "col"),
        P("blk", None),
        P("blk"),
        P(),
    )
    out_specs = (P("blk", "col", None), P("blk", "col", None))
    return jax.shard_map(
        functools.partial(local, mesh.shape["blk"], mesh.shape["col"]),
        mesh=mesh, in_specs=in_specs, out_specs=out_specs, check_vma=False)
```

profile of v0, /device:TPU:8, one launch (start us, length us, event | category | flops | bytes accessed | tf_op | source)
XLA Modules:
  0.0 98.0 jit_solution(12538189257245056835)
XLA Ops:
  0.6 0.0 copy-start.1
  0.6 1.3 %pad_convert_fusion.smass_ref = f32[8,256]{1,0:T(8,128)} fusion(bf16[2,256]{1,0:T(2,128)(2,1)} %param.9), kind=kLoop, calls=%fused_computation | loop fusion | flops 2048 | bytes 9216 | tf_op jit(solution)/shard_map/jit(_pad)/pad | solution.py:242
  1.9 0.0 copy-done.1
  1.9 0.6 broadcast_in_dim.2.tmass_ref
  2.5 93.0 %shard_map.86 = (bf16[2,256,256]{2,1,0:T(8,128)(2,1)}, bf16[2,256,256]{2,1,0:T(8,128)(2,1)}) custom-call(bf16[2,256,256]{2,1,0:T(8,128)(2,1)} %src_ref.1, bf16[2,256,256]{2,1,0:T(8,128)(2,1)} %tgt_ref.1, f32[8,256]{1,0:T(8,128)} %pad_convert_fusion.smass_ref, f32[2,8,256]{2,1,0:T(8,128)} %broadcast_in_dim.2.tmass_ref, s32[2,8]{1,0:T(2,128)} %cand_ref.1, ...), custom_call_target="tpu_custom_call" | custom-call | flops 4831838208 | bytes 1048576 | tf_op jit(solution)/shard_map/pallas_call | solution.py:249
  95.6 0.0 copy-start
  95.6 1.7 %copy.11 = bf16[2,256,256]{2,1,0:T(8,128)(2,1)} copy(bf16[2,256,256]{2,1,0:T(8,128)(2,1)} %get-tuple-element.4) | data formatting | bytes 524288
  97.3 0.0 copy-done
  97.3 0.7 copy.12
Async XLA Ops:
  0.6 1.3 %copy-start.1 = (bf16[2,256]{1,0:T(2,128)(2,1)S(1)}, bf16[2,256]{1,0:T(2,128)(2,1)}, u32[]{:S(2)}) copy-start(bf16[2,256]{1,0:T(2,128)(2,1)} %param.10) | copy-start | bytes 3076
  95.6 1.7 %copy-start = (bf16[2,256,256]{2,1,0:T(8,128)(2,1)S(1)}, bf16[2,256,256]{2,1,0:T(8,128)(2,1)}, u32[]{:S(2)}) copy-start(bf16[2,256,256]{2,1,0:T(8,128)(2,1)} %get-tuple-element.5) | copy-start | bytes 786436
where the time goes:
time: 98.2 us; the launch traced here: 98 us
  Pallas kernels  93 us (95%)
  local copies, waits for them, and re-layouts  3.03 us (3%)
  other arithmetic  1.29 us (1%)
    pallas_call x1, Pallas kernels, local(): pl.pallas_call(functools.partial(kernel, nb_dev, nc), out_shape=(shape, s...  93 us
    unnamed x6, local copies, waits for them, and re-layouts  2.42 us

commit v1 on v0

--- a/solution.py
+++ b/solution.py
@@ -39,7 +39,7 @@
 def kernel(nb_dev, nc, src_ref, tgt_ref, smass_ref, tmass_ref, cand_ref, count_ref, home_ref,
            src_out, tgt_out, src_all, src_unit, src_turned, tgt_all, kmat, smass_all, tmass_all,
            u_rep, v_rep, row_parts, col_parts, row_tot, col_tot, back, acc, src_send, src_recv,
-           tgt_send, tgt_recv, slot_src, slot_tgt, slot_bias, pair_slot,
+           tgt_send, tgt_recv, pair_send, pair_recv, tile_unit, slot_src, slot_tgt, slot_bias, pair_slot,
            col_ss, col_rs, blk_ss, blk_rs):
     b, c = lax.axis_index("blk"), lax.axis_index("col")
     local_blocks, sub, width = src_ref.shape
@@ -65,6 +65,18 @@
             out.append(copy)
         return out
 
+    mate = b + 1 - 2 * lax.rem(b, 2)
+
+    def blk_copy(kind, d, peer, source, target):
+        copy = pltpu.make_async_remote_copy(
+            src_ref=source, dst_ref=target, send_sem=blk_ss.at[kind, d],
+            recv_sem=blk_rs.at[kind, d], device_id={"blk": peer}, device_id_type=MESH)
+        copy.start()
+        return copy
+
+    def blocks_of(index):
+        return pl.ds(index * local_blocks, local_blocks)
+
     def to_blk(kind, source, target):
         out = []
         for d in range(1, nb_dev):
@@ -82,14 +94,21 @@
 
     my_rows = pl.ds(pl.multiple_of(c * sub, sub), sub)
     my_blocks = pl.ds(b * local_blocks, local_blocks)
+    far = [
+        (d, blk_copy(0, d, lax.rem(b + d, nb_dev), tgt_ref, tgt_all.at[my_blocks]))
+        for d in range(2, nb_dev, 2)
+    ]
+    near = [blk_copy(0, 1, mate, tgt_ref, tgt_all.at[my_blocks])]
     src_copies = to_col(0, lambda peer: src_ref, src_all.at[:, my_rows, :])
-    tgt_copies = to_blk(0, lambda peer: tgt_ref, tgt_all.at[my_blocks])
-    mass_copies = to_col(1, lambda peer: smass_ref, smass_all.at[c])
-    mass_copies += to_blk(1, lambda peer: tmass_ref, tmass_all.at[my_blocks])
+    smass_all[c] = jnp.concatenate(
+        [smass_ref[...].astype(F32), jnp.zeros((8 - local_blocks, sub), F32)], axis=0)
+    masses = tmass_ref[...].astype(F32)
+    for q in range(local_blocks):
+        tmass_all[b * local_blocks + q] = jnp.broadcast_to(masses[q:q + 1], (8, sub))
+    mass_copies = to_col(1, lambda peer: smass_all.at[c], smass_all.at[c])
+    mass_copies += to_blk(1, lambda peer: tmass_all.at[my_blocks], tmass_all.at[my_blocks])
     src_all[:, my_rows, :] = src_ref[...]
     tgt_all[my_blocks] = tgt_ref[...]
-    smass_all[c] = smass_ref[...]
-    tmass_all[my_blocks] = tmass_ref[...]
 
     total = count_ref[0]
     for p in range(1, local_blocks):
@@ -116,37 +135,49 @@
             pair_slot[n, p] = found
 
     back[PAIRS] = jnp.zeros(back.shape[1:], F32)
-    acc[...] = jnp.zeros(acc.shape, F32)
-    finish(src_copies)
-
-    @pl.loop(0, nc)
-    def _(piece):
+    for d, copy in far:
+        copy.wait_recv()
+        came = blocks_of(lax.rem(b - d + nb_dev, nb_dev))
+        near.append(blk_copy(3 + ITERS, d, mate, tgt_all.at[came], tgt_all.at[came]))
+    finish(near)
+    for _, copy in far:
+        copy.wait_send()
+
+    @pl.loop(0, PAIRS)
+    def _(s):
+        tile_unit[s] = unit_rows(tgt_all[jnp.minimum(slot_tgt[s], blocks - 1)].astype(F32))
+
+    row_ids = lax.broadcasted_iota(jnp.int32, (8, full), 0)
+    block_ids = lax.broadcasted_iota(jnp.int32, (blocks, sub), 0)
+    ones = jnp.where(lax.broadcasted_iota(jnp.int32, (16, sub), 0) < 8, F32(1), F32(0)).astype(BF16)
+
+    def row_part(s, v_rows, running):
+        found = lax.dot_general(v_rows, kmat[s], NT, preferred_element_type=F32)
+        return running + jnp.where(row_ids == slot_src[s], found[:8] + found[8:], 0.0)
+
+    def score_rows(piece):
         rows = pl.ds(pl.multiple_of(piece * sub, sub), sub)
         for p in range(local_blocks):
             values = src_all[p, rows, :].astype(F32)
             src_unit[p, rows, :] = unit_rows(values)
             src_turned[p, :, rows] = jnp.transpose(values).astype(BF16)
-
-    finish(tgt_copies)
-
-    row_ids = lax.broadcasted_iota(jnp.int32, (8, full), 0)
-    block_ids = lax.broadcasted_iota(jnp.int32, (blocks, sub), 0)
-    ones = jnp.where(lax.broadcasted_iota(jnp.int32, (16, sub), 0) < 8, F32(1), F32(0)).astype(BF16)
-
-    def row_part(s, v_rows, running):
-        found = lax.dot_general(v_rows, kmat[s], NT, preferred_element_type=F32)
-        return running + jnp.where(row_ids == slot_src[s], found[:8] + found[8:], 0.0)
-
-    def first_step(s, running):
-        source, target = slot_src[s], jnp.minimum(slot_tgt[s], blocks - 1)
-        bias = slot_bias[s]
-        tile = unit_rows(tgt_all[target].astype(F32))
-        chunk = 256
-        for at in range(0, full, chunk):
-            score = lax.dot_general(src_unit[source, at:at + chunk, :], tile, NT,
+        ids = lax.broadcasted_iota(jnp.int32, (8, sub), 0)
+
+        def one(s, running):
+            source = slot_src[s]
+            score = lax.dot_general(src_unit[source, rows, :], tile_unit[s], NT,
                                     preferred_element_type=F32)
-            kmat[s, at:at + chunk, :] = jnp.exp2(score * F32(SCALE / width) + bias).astype(BF16)
-        return row_part(s, ones, running)
+            tile = jnp.exp2(score * F32(SCALE / width) + slot_bias[s]).astype(BF16)
+            kmat[s, rows, :] = tile
+            found = lax.dot_general(ones, tile, NT, preferred_element_type=F32)[:8]
+            return running + jnp.where(ids == source, found, 0.0)
+
+        row_parts[0, c, :, rows] = lax.fori_loop(0, PAIRS, one, jnp.zeros((8, sub), F32), unroll=2)
+
+    score_rows(c)
+    for d in range(1, nc):
+        src_copies[d - 1].wait()
+        score_rows(lax.rem(c - d + nc, nc))
 
     def later_step(s, running):
         return row_part(s, v_rep[jnp.minimum(slot_tgt[s], blocks - 1)], running)
@@ -157,8 +188,8 @@
         return running + jnp.where(block_ids == slot_tgt[s], found[:1], 0.0)
 
     for step in range(ITERS):
-        row_parts[step, c] = lax.fori_loop(
-            0, PAIRS, first_step if step == 0 else later_step, jnp.zeros((8, full), F32))
+        if step > 0:
+            row_parts[step, c] = lax.fori_loop(0, PAIRS, later_step, jnp.zeros((8, full), F32), unroll=4)
         finish(to_col(2 + step, lambda peer: row_parts.at[step, c], row_parts.at[step, c]))
         rows = row_parts[step, 0]
         for at in range(1, nc):
@@ -173,10 +204,10 @@
             u_rep[p] = split_rows(scaling_u[p:p + 1])
             if step == ITERS - 1:
                 src_turned[p] = (src_turned[p].astype(F32) * scaling_u[p:p + 1]).astype(BF16)
-        col_parts[step, b] = lax.fori_loop(0, PAIRS, col_step, jnp.zeros((blocks, sub), F32))
+        col_parts[step, b] = lax.fori_loop(0, PAIRS, col_step, jnp.zeros((blocks, sub), F32), unroll=4)
         col_copies = to_blk(2 + step, lambda peer: col_parts.at[step, b], col_parts.at[step, b])
         if step == ITERS - 1:
-            @pl.loop(0, PAIRS)
+            @pl.loop(0, PAIRS, unroll=2)
             def _(s):
                 back[s] = jnp.dot(src_turned[slot_src[s]], kmat[s], preferred_element_type=F32)
 
@@ -186,16 +217,17 @@
                 for p in range(1, local_blocks):
                     piece = piece + back[pair_slot[n, p]]
                 tgt_send[n] = piece.astype(BF16)
+
+            pair_sums = [
+                blk_copy(2 + ITERS, d, mate, tgt_send.at[blocks_of(lax.rem(mate + d, nb_dev))],
+                         pair_recv.at[d // 2])
+                for d in range(0, nb_dev, 2)
+            ]
         finish(col_copies)
         columns = col_parts[step, 0]
         for at in range(1, nb_dev):
             columns = columns + col_parts[step, at]
         col_tot[...] = columns
-        if step == ITERS - 1:
-            tgt_sums = to_blk(
-                2 + ITERS, lambda peer: tgt_send.at[pl.ds(peer * local_blocks, local_blocks)],
-                tgt_recv.at[b])
-
         @pl.loop(0, blocks)
         def _(n):
             row = tmass_all[n, :1, :] / col_tot[pl.ds(n, 1), :]
@@ -204,32 +236,51 @@
             else:
                 tgt_all[n] = (tgt_all[n].astype(F32) * column_of(row, width)).astype(BF16)
 
-    @pl.loop(0, PAIRS)
-    def _(s):
-        tile = tgt_all[jnp.minimum(slot_tgt[s], blocks - 1)]
-        source = slot_src[s]
-        chunk = 256
-        for at in range(0, full, chunk):
-            toward = jnp.dot(kmat[s, at:at + chunk, :], tile, preferred_element_type=F32)
+    def toward_rows(piece):
+        rows = pl.ds(pl.multiple_of(piece * sub, sub), sub)
+        acc[...] = jnp.zeros(acc.shape, F32)
+
+        @pl.loop(0, PAIRS, unroll=2)
+        def _(s):
+            tile = tgt_all[jnp.minimum(slot_tgt[s], blocks - 1)]
+            toward = jnp.dot(kmat[s, rows, :], tile, preferred_element_type=F32)
             for p in range(local_blocks):
-                hot = jnp.where(source == p, F32(1), F32(0))
-                acc[p, at:at + chunk, :] += toward * hot
-
-    for at in range(nc):
-        src_send[at] = acc[:, at * sub:(at + 1) * sub, :].astype(BF16)
-    src_sums = to_col(2 + ITERS, lambda peer: src_send.at[peer], src_recv.at[c])
-    src_recv[c] = src_send[c]
-    tgt_recv[b] = tgt_send[my_blocks]
+                acc[p] += toward * jnp.where(slot_src[s] == p, F32(1), F32(0))
+
+    src_sums = []
+    for d in range(nc - 1, 0, -1):
+        peer = lax.rem(c + d, nc)
+        toward_rows(peer)
+        src_send[d] = acc[...].astype(BF16)
+        copy = pltpu.make_async_remote_copy(
+            src_ref=src_send.at[d], dst_ref=src_recv.at[d], send_sem=col_ss.at[2 + ITERS, d],
+            recv_sem=col_rs.at[2 + ITERS, d], device_id={"col": peer}, device_id_type=MESH)
+        copy.start()
+        src_sums.append(copy)
+    tgt_sums = []
+    for d in range(2, nb_dev, 2):
+        peer = lax.rem(b + d, nb_dev)
+        pair_sums[d // 2].wait_recv()
+        pair_send[d // 2] = (tgt_send[blocks_of(peer)].astype(F32)
+                             + pair_recv[d // 2].astype(F32)).astype(BF16)
+        tgt_sums.append(blk_copy(4 + ITERS, d, peer, pair_send.at[d // 2],
+                                 tgt_recv.at[d // 2]))
+    pair_sums[0].wait_recv()
+
+
+    toward_rows(c)
     finish(src_sums)
     for p in range(local_blocks):
-        whole = src_recv[0, p].astype(F32)
+        whole = acc[p]
         for at in range(1, nc):
             whole = whole + src_recv[at, p].astype(F32)
         src_out[p] = (whole / column_of(row_tot[p:p + 1, my_rows], width)).astype(BF16)
     finish(tgt_sums)
+    for copy in pair_sums:
+        copy.wait_send()
     for q in range(local_blocks):
-        whole = tgt_recv[0, q].astype(F32)
-        for at in range(1, nb_dev):
+        whole = (tgt_send[b * local_blocks + q].astype(F32) + pair_recv[0, q].astype(F32))
+        for at in range(1, nb_dev // 2):
             whole = whole + tgt_recv[at, q].astype(F32)
         whole = whole / col_tot[pl.ds(b * local_blocks + q, 1), :]
         tgt_out[q] = jnp.transpose(whole).astype(BF16)
@@ -239,8 +290,6 @@
     local_blocks, sub, width = src_feat.shape
     blocks = tgt_home.shape[0]
     full = sub * nc
-    smass = jnp.pad(src_mass.astype(F32), ((0, 8 - local_blocks), (0, 0)))
-    tmass = jnp.broadcast_to(tgt_mass.astype(F32)[:, None, :], (local_blocks, 8, sub))
     vmem = pl.BlockSpec(memory_space=pltpu.VMEM)
     smem = pl.BlockSpec(memory_space=pltpu.SMEM)
     kinds = 3 + ITERS
@@ -266,26 +315,29 @@
             pltpu.VMEM((8, full), F32),
             pltpu.VMEM((blocks, sub), F32),
             pltpu.VMEM((PAIRS + 1, width, sub), F32),
-            pltpu.VMEM((local_blocks, full, width), F32),
+            pltpu.VMEM((local_blocks, sub, width), F32),
             pltpu.VMEM((nc, local_blocks, sub, width), BF16),
             pltpu.VMEM((nc, local_blocks, sub, width), BF16),
             pltpu.VMEM((blocks, width, sub), BF16),
-            pltpu.VMEM((nb_dev, local_blocks, width, sub), BF16),
+            pltpu.VMEM((nb_dev // 2, local_blocks, width, sub), BF16),
+            pltpu.VMEM((nb_dev // 2, local_blocks, width, sub), BF16),
+            pltpu.VMEM((nb_dev // 2, local_blocks, width, sub), BF16),
+            pltpu.VMEM((PAIRS, sub, width), BF16),
             pltpu.SMEM((PAIRS,), jnp.int32),
             pltpu.SMEM((PAIRS,), jnp.int32),
             pltpu.SMEM((PAIRS,), F32),
             pltpu.SMEM((blocks, local_blocks), jnp.int32),
             pltpu.SemaphoreType.DMA((kinds, nc)),
             pltpu.SemaphoreType.DMA((kinds, nc)),
-            pltpu.SemaphoreType.DMA((kinds, nb_dev)),
-            pltpu.SemaphoreType.DMA((kinds, nb_dev)),
+            pltpu.SemaphoreType.DMA((kinds + 2, nb_dev)),
+            pltpu.SemaphoreType.DMA((kinds + 2, nb_dev)),
         ],
         compiler_params=pltpu.CompilerParams(
             collective_id=0, has_side_effects=True, vmem_limit_bytes=56 * 1024 * 1024),
         cost_estimate=pl.CostEstimate(
             flops=flops, bytes_accessed=4 * local_blocks * sub * width * 2,
             transcendentals=PAIRS * full * sub),
-    )(src_feat, tgt_feat, smass, tmass, candidates, counts, tgt_home)
+    )(src_feat, tgt_feat, src_mass, tgt_mass, candidates, counts, tgt_home)
 
 
 def solution(mesh):

time: 98.2 us -> 90.3 us (0.920)
  the two profiles are of different devices: /device:TPU:8 before, /device:TPU:0 now
where the time goes in v1:
time: 90.3 us; the launch traced here: 90.1 us
  Pallas kernels  87 us (96%)
  local copies, waits for them, and re-layouts  2.42 us (3%)
    pallas_call x1, Pallas kernels, local(): pl.pallas_call(functools.partial(kernel, nb_dev, nc), out_shape=(shape, s...  87 us
    unnamed x4, local copies, waits for them, and re-layouts  2.42 us

profile of v1, /device:TPU:0, one launch (start us, length us, event | category | flops | bytes accessed | tf_op | source)
XLA Modules:
  0.0 90.1 jit_solution(17971742982822100305)
XLA Ops:
  0.6 87.0 %shard_map.86 = (bf16[2,256,256]{2,1,0:T(8,128)(2,1)}, bf16[2,256,256]{2,1,0:T(8,128)(2,1)}) custom-call(bf16[2,256,256]{2,1,0:T(8,128)(2,1)} %src_ref.1, bf16[2,256,256]{2,1,0:T(8,128)(2,1)} %tgt_ref.1, bf16[2,256]{1,0:T(2,128)(2,1)} %smass_ref.1, bf16[2,256]{1,0:T(2,128)(2,1)} %tmass_ref.1, s32[2,8]{1,0:T(2,128)} %cand_ref.1, s32[2]{0:T(128)} %count_ref.1, ...), custom_call_target="tpu_custom_call" | custom-call | flops 4831838208 | bytes 1048576 | tf_op jit(solution)/shard_map/pallas_call | solution.py:298
  87.7 0.0 copy-start
  87.7 1.7 %copy.11 = bf16[2,256,256]{2,1,0:T(8,128)(2,1)} copy(bf16[2,256,256]{2,1,0:T(8,128)(2,1)} %get-tuple-element.4) | data formatting | bytes 524288
  89.4 0.0 copy-done
  89.4 0.7 copy.12
Async XLA Ops:
  87.7 1.7 %copy-start = (bf16[2,256,256]{2,1,0:T(8,128)(2,1)S(1)}, bf16[2,256,256]{2,1,0:T(8,128)(2,1)}, u32[]{:S(2)}) copy-start(bf16[2,256,256]{2,1,0:T(8,128)(2,1)} %get-tuple-element.5) | copy-start | bytes 786436

commit v2 on v1

--- a/solution.py
+++ b/solution.py
@@ -143,7 +143,7 @@
     for _, copy in far:
         copy.wait_send()
 
-    @pl.loop(0, PAIRS)
+    @pl.loop(0, PAIRS, unroll=4)
     def _(s):
         tile_unit[s] = unit_rows(tgt_all[jnp.minimum(slot_tgt[s], blocks - 1)].astype(F32))
 
@@ -172,7 +172,7 @@
             found = lax.dot_general(ones, tile, NT, preferred_element_type=F32)[:8]
             return running + jnp.where(ids == source, found, 0.0)
 
-        row_parts[0, c, :, rows] = lax.fori_loop(0, PAIRS, one, jnp.zeros((8, sub), F32), unroll=2)
+        row_parts[0, c, :, rows] = lax.fori_loop(0, PAIRS, one, jnp.zeros((8, sub), F32), unroll=6)
 
     score_rows(c)
     for d in range(1, nc):
@@ -189,7 +189,7 @@
 
     for step in range(ITERS):
         if step > 0:
-            row_parts[step, c] = lax.fori_loop(0, PAIRS, later_step, jnp.zeros((8, full), F32), unroll=4)
+            row_parts[step, c] = lax.fori_loop(0, PAIRS, later_step, jnp.zeros((8, full), F32), unroll=12)
         finish(to_col(2 + step, lambda peer: row_parts.at[step, c], row_parts.at[step, c]))
         rows = row_parts[step, 0]
         for at in range(1, nc):
@@ -204,14 +204,14 @@
             u_rep[p] = split_rows(scaling_u[p:p + 1])
             if step == ITERS - 1:
                 src_turned[p] = (src_turned[p].astype(F32) * scaling_u[p:p + 1]).astype(BF16)
-        col_parts[step, b] = lax.fori_loop(0, PAIRS, col_step, jnp.zeros((blocks, sub), F32), unroll=4)
+        col_parts[step, b] = lax.fori_loop(0, PAIRS, col_step, jnp.zeros((blocks, sub), F32), unroll=12)
         col_copies = to_blk(2 + step, lambda peer: col_parts.at[step, b], col_parts.at[step, b])
         if step == ITERS - 1:
-            @pl.loop(0, PAIRS, unroll=2)
+            @pl.loop(0, PAIRS, unroll=4)
             def _(s):
                 back[s] = jnp.dot(src_turned[slot_src[s]], kmat[s], preferred_element_type=F32)
 
-            @pl.loop(0, blocks)
+            @pl.loop(0, blocks, unroll=2)
             def _(n):
                 piece = back[pair_slot[n, 0]]
                 for p in range(1, local_blocks):
@@ -228,7 +228,7 @@
         for at in range(1, nb_dev):
             columns = columns + col_parts[step, at]
         col_tot[...] = columns
-        @pl.loop(0, blocks)
+        @pl.loop(0, blocks, unroll=8)
         def _(n):
             row = tmass_all[n, :1, :] / col_tot[pl.ds(n, 1), :]
             if step < ITERS - 1:
@@ -240,7 +240,7 @@
         rows = pl.ds(pl.multiple_of(piece * sub, sub), sub)
         acc[...] = jnp.zeros(acc.shape, F32)
 
-        @pl.loop(0, PAIRS, unroll=2)
+        @pl.loop(0, PAIRS, unroll=4)
         def _(s):
             tile = tgt_all[jnp.minimum(slot_tgt[s], blocks - 1)]
             toward = jnp.dot(kmat[s, rows, :], tile, preferred_element_type=F32)

time: 90.3 us -> 85.4 us (0.946)
  Pallas kernels: 87 us -> 82.1 us
    pallas_call x1, Pallas kernels: 87 us -> 82.1 us  [local(): pl.pallas_call(functools.partial(kernel, nb_dev, nc), out_shape=(shape, s...]
where the time goes in v2:
time: 85.4 us; the launch traced here: 85.2 us
  Pallas kernels  82.1 us (96%)
  local copies, waits for them, and re-layouts  2.42 us (3%)
    pallas_call x1, Pallas kernels, local(): pl.pallas_call(functools.partial(kernel, nb_dev, nc), out_shape=(shape, s...  82.1 us
    unnamed x4, local copies, waits for them, and re-layouts  2.42 us

profile of v2, /device:TPU:0, one launch (start us, length us, event | category | flops | bytes accessed | tf_op | source)
XLA Modules:
  0.0 85.2 jit_solution(11483305626224592008)
XLA Ops:
  0.6 82.1 %shard_map.86 = (bf16[2,256,256]{2,1,0:T(8,128)(2,1)}, bf16[2,256,256]{2,1,0:T(8,128)(2,1)}) custom-call(bf16[2,256,256]{2,1,0:T(8,128)(2,1)} %src_ref.1, bf16[2,256,256]{2,1,0:T(8,128)(2,1)} %tgt_ref.1, bf16[2,256]{1,0:T(2,128)(2,1)} %smass_ref.1, bf16[2,256]{1,0:T(2,128)(2,1)} %tmass_ref.1, s32[2,8]{1,0:T(2,128)} %cand_ref.1, s32[2]{0:T(128)} %count_ref.1, ...), custom_call_target="tpu_custom_call" | custom-call | flops 4831838208 | bytes 1048576 | tf_op jit(solution)/shard_map/pallas_call | solution.py:298
  82.8 0.0 copy-start
  82.8 1.7 %copy.11 = bf16[2,256,256]{2,1,0:T(8,128)(2,1)} copy(bf16[2,256,256]{2,1,0:T(8,128)(2,1)} %get-tuple-element.4) | data formatting | bytes 524288
  84.5 0.0 copy-done
  84.5 0.7 copy.12
Async XLA Ops:
  82.8 1.7 %copy-start = (bf16[2,256,256]{2,1,0:T(8,128)(2,1)S(1)}, bf16[2,256,256]{2,1,0:T(8,128)(2,1)}, u32[]{:S(2)}) copy-start(bf16[2,256,256]{2,1,0:T(8,128)(2,1)} %get-tuple-element.5) | copy-start | bytes 786436
